TPU v7x, 256 devices: a whole 4x4x8 slice. The times are simulated.
256 devices in a mesh: row: 8 (over z), col: 32 (over x, y, core).
Axes of the slice: x: 4, y: 4, z: 8, core: 2. Of those that a mesh axis runs over, the one named last changes fastest.
Arguments:
- block_input: bfloat16 [1024, 8192], P('col', 'row'), may hold values from -6 to 6
- output_grad: bfloat16 [1024, 8192], P('col', 'row'), may hold values from -1.5 to 1.5
- gate_pre: bfloat16 [1024, 28672], P('row', 'col'), may hold values from -6 to 6
- up_pre: bfloat16 [1024, 28672], P('row', 'col'), may hold values from -6 to 6
- w_gate: bfloat16 [8192, 28672], P('row', 'col'), may hold values from -0.0625 to 0.0625
- w_up: bfloat16 [8192, 28672], P('row', 'col'), may hold values from -0.0625 to 0.0625
- w_down: bfloat16 [28672, 8192], P('col', 'row'), may hold values from -0.03125 to 0.03125
Outputs:
- grad_input: bfloat16 [1024, 8192], P('col', 'row')
- grad_gate: bfloat16 [8192, 28672], P('row', 'col')
- grad_up: bfloat16 [8192, 28672], P('row', 'col')
- grad_down: bfloat16 [28672, 8192], P('col', 'row')
All inputs are finite; a program needn't handle non-finite values.
Results may differ from a plain program's by a relative error of at most 0.027.
Values may be sent and summed in bfloat16 or wider, within the bound.
A program may use at most 64 MiB of HBM per device.

v0:
```python
import jax
import jax.numpy as jnp
from jax import lax
from jax.sharding import PartitionSpec as P


def swiglu_grad(upstream, gate_pre, up_pre):
    gate_vals = gate_pre.astype(jnp.float32)
    up_vals = up_pre.astype(jnp.float32)
    sigmoid_gate = jax.nn.sigmoid(gate_vals)
    silu_value = gate_vals * sigmoid_gate
    activated = (silu_value * up_vals).astype(jnp.bfloat16)
    up_delta = (upstream * silu_value).astype(jnp.bfloat16)
    gate_delta = (
        upstream * up_vals * sigmoid_gate * (1.0 + gate_vals * (1.0 - sigmoid_gate))
    ).astype(jnp.bfloat16)
    return (activated, gate_delta, up_delta)


def contract_rows(left, right):
    return lax.dot_general(
        left, right, (((0,), (0,)), ((), ())), preferred_element_type=jnp.float32
    )


def contract_cols(left, right):
    return lax.dot_general(
        left, right, (((1,), (1,)), ((), ())), preferred_element_type=jnp.float32
    )


def on_device(block_input, output_grad, gate_pre, up_pre, w_gate, w_up, w_down):
    output_all, input_all = (
        lax.all_gather(output_grad, "col", axis=0, tiled=True),
        lax.all_gather(block_input, "col", axis=0, tiled=True),
    )
    upstream = lax.psum_scatter(
        contract_cols(output_all, w_down).astype(jnp.bfloat16),
        "row",
        scatter_dimension=0,
        tiled=True,
    ).astype(jnp.float32)
    derived = swiglu_grad(upstream, gate_pre, up_pre)
    activated = lax.all_gather(derived[0], "row", axis=0, tiled=True)
    gate_delta = lax.all_gather(derived[1], "row", axis=0, tiled=True)
    up_delta = lax.all_gather(derived[2], "row", axis=0, tiled=True)
    sum_gate = contract_rows(input_all, gate_delta)
    sum_up = contract_rows(input_all, up_delta)
    sum_down = contract_rows(activated, output_all)
    block_rows = contract_cols(gate_delta, w_gate) + contract_cols(up_delta, w_up)
    input_part = block_rows
    sum_gate, sum_up, sum_down, input_part = (sum_gate, sum_up, sum_down, input_part)
    grad_input = lax.psum_scatter(
        input_part.astype(jnp.bfloat16), "col", scatter_dimension=0, tiled=True
    )
    return (
        grad_input,
        sum_gate.astype(jnp.bfloat16),
        sum_up.astype(jnp.bfloat16),
        sum_down.astype(jnp.bfloat16),
    )


def solution(mesh):
    return jax.shard_map(
        on_device,
        mesh=mesh,
        in_specs=(
            P("col", "row"),
            P("col", "row"),
            P("row", "col"),
            P("row", "col"),
            P("row", "col"),
            P("row", "col"),
            P("col", "row"),
        ),
        out_specs=(P("col", "row"), P("row", "col"), P("row", "col"), P("col", "row")),
        check_vma=False,
    )
```

profile of v0, /device:TPU:4, one launch (start us, length us, event | category | flops | bytes accessed | tf_op | source)
XLA Modules:
  0.0 379.4 jit_solution(14288515406929489246)
XLA Ops:
  7.2 0.0 copy-start
  7.2 0.0 all-gather.6.cloned.1.call-start
  7.2 0.7 all-gather.6.cloned.1.call-update
  7.9 0.0 reduce-scatter.3.cloned.1.call-start
  8.0 53.9 %all-gather.6.cloned.1.call-done = bf16[1024,1024]{1,0:T(8,128)(2,1)} async-done(((bf16[32,1024]{1,0:T(8,128)(2,1)}), bf16[1024,1024]{1,0:T(8,128)(2,1)}) %all-gather.6.cloned.1.call-update) | async-done | bytes 2097168 | tf_op jit(solution)/shard_map/all_gather | solution.py:34
  61.8 5.7 %convolution_convert_fusion.1 = bf16[1024,896]{1,0:T(8,128)(2,1)} fusion(bf16[1024,1024]{1,0:T(8,128)(2,1)} %all-gather.6.cloned.1.call-done, bf16[896,1024]{1,0:T(8,128)(2,1)} %param.13), kind=kOutput, calls=%fused_computation.4 | convolution fusion | flops 1879965696 | bytes 5767168 | tf_op jit(solution)/shard_map/dot_general | solution.py:27
  67.6 0.0 copy-start.1
  67.6 0.0 copy-start.2
  67.6 0.0 reduce-scatter.3.cloned.1.call-update
  67.6 0.0 all-gather.8.cloned.1.call-start
  67.6 41.1 %reduce-scatter.3.cloned.1.call-done = bf16[128,896]{1,0:T(8,128)(2,1)} async-done(((bf16[1024,896]{1,0:T(8,128)(2,1)}), bf16[128,896]{1,0:T(8,128)(2,1)}) %reduce-scatter.3.cloned.1.call-update) | async-done | bytes 229392 | tf_op jit(solution)/shard_map/reduce_scatter | solution.py:37
  108.8 0.0 copy-done.1
  108.8 0.0 copy-done.2
  108.8 2.0 fusion.4
  110.8 0.0 all-gather.8.cloned.1.call-update
  110.8 0.0 all-gather.10.cloned.1.call-start
  110.9 0.5 all-gather.10.cloned.1.call-update
  111.4 0.0 all-gather.12.cloned.1.call-start
  111.5 0.5 all-gather.12.cloned.1.call-update
  112.0 0.0 all-gather.14.cloned.1.call-start
  112.0 0.5 all-gather.14.cloned.1.call-update
  112.6 0.0 reduce-scatter.5.cloned.1.call-start
  112.6 38.0 %all-gather.8.cloned.1.call-done = bf16[1024,896]{1,0:T(8,128)(2,1)} async-done(((bf16[128,896]{1,0:T(8,128)(2,1)}), bf16[1024,896]{1,0:T(8,128)(2,1)}) %all-gather.8.cloned.1.call-update) | async-done | bytes 1835024 | tf_op jit(solution)/shard_map/all_gather | solution.py:45
  150.6 0.0 copy-done
  150.6 5.8 %fusion.9 = f32[1024,1024]{1,0:T(8,128)} fusion(bf16[1024,896]{1,0:T(8,128)(2,1)} %all-gather.8.cloned.1.call-done, bf16[1024,896]{1,0:T(8,128)(2,1)S(1)} %copy-done), kind=kOutput, calls=%fused_computation.20 | convolution fusion | flops 1879048192 | bytes 7864320 | tf_op jit(solution)/shard_map/dot_general | solution.py:27
  156.4 35.6 %all-gather.10.cloned.1.call-done = bf16[1024,896]{1,0:T(8,128)(2,1)} async-done(((bf16[128,896]{1,0:T(8,128)(2,1)}), bf16[1024,896]{1,0:T(8,128)(2,1)}) %all-gather.10.cloned.1.call-update) | async-done | bytes 1835024 | tf_op jit(solution)/shard_map/all_gather | solution.py:46
  192.0 7.0 %add_convert_fusion = bf16[1024,1024]{1,0:T(8,128)(2,1)} fusion(f32[1024,1024]{1,0:T(8,128)} %fusion.9, bf16[1024,896]{1,0:T(8,128)(2,1)} %all-gather.10.cloned.1.call-done, bf16[1024,896]{1,0:T(8,128)(2,1)} %param.12), kind=kOutput, calls=%fused_computation | convolution fusion | flops 1881145344 | bytes 9961472 | tf_op jit(solution)/shard_map/dot_general | solution.py:27
  199.1 0.0 reduce-scatter.5.cloned.1.call-update
  199.1 42.3 %all-gather.12.cloned.1.call-done = bf16[1024,1024]{1,0:T(8,128)(2,1)} async-done(((bf16[32,1024]{1,0:T(8,128)(2,1)}), bf16[1024,1024]{1,0:T(8,128)(2,1)}) %all-gather.12.cloned.1.call-update) | async-done | bytes 2097168 | tf_op jit(solution)/shard_map/all_gather | solution.py:35
  241.4 5.5 %convert_bitcast_fusion.1 = bf16[1024,896]{0,1:T(8,128)(2,1)} fusion(bf16[1024,896]{1,0:T(8,128)(2,1)} %all-gather.8.cloned.1.call-done, bf16[1024,1024]{1,0:T(8,128)(2,1)} %all-gather.12.cloned.1.call-done), kind=kOutput, calls=%fused_computation.2 | convolution fusion | flops 1879965696 | bytes 5767168 | tf_op jit(solution)/shard_map/dot_general | solution.py:21
  246.8 3.8 %copy.11 = bf16[1024,896]{1,0:T(8,128)(2,1)} copy(bf16[1024,896]{0,1:T(8,128)(2,1)} %convert_bitcast_fusion.1) | data formatting | bytes 3670016
  250.6 5.5 %convert_bitcast_fusion = bf16[1024,896]{0,1:T(8,128)(2,1)} fusion(bf16[1024,896]{1,0:T(8,128)(2,1)} %all-gather.10.cloned.1.call-done, bf16[1024,1024]{1,0:T(8,128)(2,1)} %all-gather.12.cloned.1.call-done), kind=kOutput, calls=%fused_computation.1 | convolution fusion | flops 1879965696 | bytes 5767168 | tf_op jit(solution)/shard_map/dot_general | solution.py:21
  256.1 3.8 %copy.12 = bf16[1024,896]{1,0:T(8,128)(2,1)} copy(bf16[1024,896]{0,1:T(8,128)(2,1)} %convert_bitcast_fusion) | data formatting | bytes 3670016
  259.9 23.6 %all-gather.14.cloned.1.call-done = bf16[1024,896]{1,0:T(8,128)(2,1)} async-done(((bf16[128,896]{1,0:T(8,128)(2,1)}), bf16[1024,896]{1,0:T(8,128)(2,1)}) %all-gather.14.cloned.1.call-update) | async-done | bytes 1835024 | tf_op jit(solution)/shard_map/all_gather | solution.py:44
  283.5 5.5 %convolution_convert_fusion = bf16[896,1024]{1,0:T(8,128)(2,1)} fusion(bf16[1024,896]{1,0:T(8,128)(2,1)} %all-gather.14.cloned.1.call-done, bf16[1024,1024]{1,0:T(8,128)(2,1)} %all-gather.6.cloned.1.call-done), kind=kOutput, calls=%fused_computation.3 | convolution fusion | flops 1879965696 | bytes 5767168 | tf_op jit(solution)/shard_map/dot_general | solution.py:21
  288.9 83.6 %reduce-scatter.5.cloned.1.call-done = bf16[32,1024]{1,0:T(8,128)(2,1)} async-done(((bf16[1024,1024]{1,0:T(8,128)(2,1)}), bf16[32,1024]{1,0:T(8,128)(2,1)}) %reduce-scatter.5.cloned.1.call-update) | async-done | bytes 65552 | tf_op jit(solution)/shard_map/reduce_scatter | solution.py:53
Async XLA Ops:
  7.2 143.5 %copy-start = (bf16[1024,896]{1,0:T(8,128)(2,1)S(1)}, bf16[1024,896]{1,0:T(8,128)(2,1)}, u32[]{:S(2)}) copy-start(bf16[1024,896]{1,0:T(8,128)(2,1)} %param.11) | copy-start | bytes 5505028
  7.2 54.6 %all-gather.6.cloned.1.call-start = ((), (), s32[]{:S(2)}) async-start(), calls=%async_computation.2 | async-start | bytes 2162688 | tf_op jit(solution)/shard_map/all_gather | solution.py:34
  7.9 100.9 %reduce-scatter.3.cloned.1.call-start = ((), (), s32[]{:S(2)}) async-start(), calls=%async_computation.3 | async-start | bytes 2064384 | tf_op jit(solution)/shard_map/reduce_scatter | solution.py:37
  67.6 41.2 %copy-start.1 = (bf16[128,896]{1,0:T(8,128)(2,1)S(1)}, bf16[128,896]{1,0:T(8,128)(2,1)}, u32[]{:S(2)}) copy-start(bf16[128,896]{1,0:T(8,128)(2,1)} %param.10) | copy-start | bytes 688132
  67.6 41.2 %copy-start.2 = (bf16[128,896]{1,0:T(8,128)(2,1)S(1)}, bf16[128,896]{1,0:T(8,128)(2,1)}, u32[]{:S(2)}) copy-start(bf16[128,896]{1,0:T(8,128)(2,1)} %param.9) | copy-start | bytes 688132
  67.6 83.0 %all-gather.8.cloned.1.call-start = ((), (), s32[]{:S(2)}) async-start(), calls=%async_computation.4 | async-start | bytes 2064384 | tf_op jit(solution)/shard_map/all_gather | solution.py:45
  110.8 81.2 %all-gather.10.cloned.1.call-start = ((), (), s32[]{:S(2)}) async-start(), calls=%async_computation.5 | async-start | bytes 2064384 | tf_op jit(solution)/shard_map/all_gather | solution.py:46
  111.4 130.0 %all-gather.12.cloned.1.call-start = ((), (), s32[]{:S(2)}) async-start(), calls=%async_computation.7 | async-start | bytes 2162688 | tf_op jit(solution)/shard_map/all_gather | solution.py:35
  112.0 171.5 %all-gather.14.cloned.1.call-start = ((), (), s32[]{:S(2)}) async-start(), calls=%async_computation.8 | async-start | bytes 2064384 | tf_op jit(solution)/shard_map/all_gather | solution.py:44
  112.6 259.9 %reduce-scatter.5.cloned.1.call-start = ((), (), s32[]{:S(2)}) async-start(), calls=%async_computation.6 | async-start | bytes 2162688 | tf_op jit(solution)/shard_map/reduce_scatter | solution.py:53
Sparse Core Ops, SparseCore 0:
  10.6 51.2 all-gather.5
  67.7 41.0 reduce-scatter.2
  111.1 39.4 all-gather.7
  152.8 39.1 all-gather.9
  194.4 46.8 all-gather.11
  243.0 40.4 all-gather.13
  287.9 84.5 reduce-scatter.4
where the time goes:
time: 380 us; the launch traced here: 379 us
  waiting for transfers between devices  320 us (84%)
  matrix products  35 us (9%)
  between operations  14.1 us (4%)
  local copies, waits for them, and re-layouts  7.61 us (2%)
    reduce_scatter x1, waiting for transfers between devices, on_device(): lax.psum_scatter(input_part.astype(jnp.bfloat16), 'col', scatter_dimensio...  83.6 us
    all_gather x1, waiting for transfers between devices, on_device(): lax.all_gather(output_grad, 'col', axis=0, tiled=True)  53.9 us
    all_gather x1, waiting for transfers between devices, on_device(): lax.all_gather(block_input, 'col', axis=0, tiled=True)  42.3 us
    reduce_scatter x1, waiting for transfers between devices, on_device(): lax.psum_scatter(contract_cols(output_all, w_down).astype(jnp.bfloat16),...  41.1 us
    all_gather x1, waiting for transfers between devices, on_device(): gate_delta = lax.all_gather(derived[1], 'row', axis=0, tiled=True)  38 us
    all_gather x1, waiting for transfers between devices, on_device(): up_delta = lax.all_gather(derived[2], 'row', axis=0, tiled=True)  35.6 us
    all_gather x1, waiting for transfers between devices, on_device(): activated = lax.all_gather(derived[0], 'row', axis=0, tiled=True)  23.6 us
    dot_general x3, matrix products, contract_cols(): lax.dot_general(left, right, (((1,), (1,)), ((), ())), preferred_element_...  18.6 us
  transfers between devices with their start and end apart: 7, of which 7 were waited for; matrix products, arithmetic and copies ran while one was open for 10% of the time, Pallas kernels for 0%

commit v1 on v0

v1 whole, which is shorter than its diff:
```python
import functools

import jax
import jax.numpy as jnp
from jax import lax
from jax.experimental import pallas as pl
from jax.experimental.pallas import tpu as pltpu
from jax.sharding import PartitionSpec as P

MESH = pl.DeviceIdType.MESH
BF, F32 = jnp.bfloat16, jnp.float32
NZ, NCHIP = 8, 16
TB = 128
DB = 1024
FB = 896
PR = 32


def nt(a, b):
    return lax.dot_general(a, b, (((1,), (1,)), ((), ())), preferred_element_type=F32)


def nn(a, b):
    return lax.dot_general(a, b, (((1,), (0,)), ((), ())), preferred_element_type=F32)


def kernel(
    x_h, og_h, g_h, u_h, wg_h, wu_h, wd_h,
    gi_h, gg_h, gu_h, gdn_h,
    og, xa, xt, gv, uv, wg, wu, wd, actt, dl, terms, rs_out, rs_in, acc, stage, gdn, own, cs, cr, sx, rr, gi,
    loc, act_s, act_r, og_s, og_r, ogc_s, ogc_r, x_s, x_r, xc_s, xc_r, rs_s, rs_r, ag_s, ag_r, cs_s, cs_r, rr_s, rr_r, outs,
):
    z, col = lax.axis_index("row"), lax.axis_index("col")
    chip, core = col // 2, lax.rem(col, 2)
    sib = (z, col + 1 - 2 * core)

    def zdev(d):
        return (lax.rem(z + (1 if d == 0 else NZ - 1), NZ), col)

    def zrel(n):
        return lax.rem(z + (n % NZ), NZ)

    def chip_at(j):
        return lax.rem(chip + j + NCHIP, NCHIP)

    def chip_dev(j):
        return (z, 2 * chip_at(j) + core)

    def remote(src, dst, ss, rs, dev):
        return pltpu.make_async_remote_copy(
            src_ref=src, dst_ref=dst, send_sem=ss, recv_sem=rs, device_id=dev, device_id_type=MESH
        )

    mine = pl.ds(pl.multiple_of(col * PR, PR), PR)
    locals_ = [
        pltpu.make_async_copy(og_h, og.at[mine], loc.at[0]),
        pltpu.make_async_copy(g_h, gv, loc.at[1]),
        pltpu.make_async_copy(u_h, uv, loc.at[2]),
        pltpu.make_async_copy(x_h, xa.at[mine], loc.at[3]),
        pltpu.make_async_copy(wd_h, wd, loc.at[4]),
        pltpu.make_async_copy(wg_h, wg, loc.at[5]),
        pltpu.make_async_copy(wu_h, wu, loc.at[6]),
    ]
    for c in locals_:
        c.start()

    bar = pltpu.get_barrier_semaphore()
    for d in (0, 1):
        pl.semaphore_signal(bar, inc=1, device_id=zdev(d), device_id_type=MESH)
    pl.semaphore_signal(bar, inc=1, device_id=sib, device_id_type=MESH)

    def greet(j, _):
        pl.semaphore_signal(bar, inc=1, device_id=chip_dev(j), device_id_type=MESH)
        return 0

    lax.fori_loop(1, NCHIP, greet, 0)
    pl.semaphore_wait(bar, NCHIP + 2)

    def piece(buf, j):
        return buf.at[pl.ds(pl.multiple_of((2 * chip_at(j) + core) * PR, PR), PR)]

    def spread(buf, j, ss, rs):
        return remote(buf.at[mine], buf.at[mine], ss.at[j], rs.at[j], chip_dev(j))

    def landed(buf, j, ss, rs):
        p = piece(buf, NCHIP - j)
        return remote(p, p, ss.at[j], rs.at[j], chip_dev(j))

    def share(buf, j, ss, rs):
        p = piece(buf, NCHIP - j)
        return remote(p, p, ss.at[j], rs.at[j], sib)

    def shared(buf, j, ss, rs):
        p = buf.at[pl.ds(pl.multiple_of((2 * chip_at(NCHIP - j) + 1 - core) * PR, PR), PR)]
        return remote(p, p, ss.at[j], rs.at[j], sib)

    def send_own(buf, s, r, cs_, cr_):
        def body(j, _):
            spread(buf, j, s, r).start()
            return 0

        lax.fori_loop(1, NCHIP, body, 0)
        share(buf, 0, cs_, cr_).start()

    def pass_on(lo, hi, buf, s, r, cs_, cr_):
        def body(j, _):
            landed(buf, j, s, r).wait_recv()
            share(buf, j, cs_, cr_).start()
            return 0

        lax.fori_loop(lo, hi, body, 0)

    def wait_shared(buf, cs_, cr_):
        def body(j, _):
            shared(buf, j, cs_, cr_).wait_recv()
            return 0

        lax.fori_loop(0, NCHIP, body, 0)

    ogx, xx = (og, og_s, og_r, ogc_s, ogc_r), (xa, x_s, x_r, xc_s, xc_r)

    locals_[0].wait()
    send_own(*ogx)

    def hops(d, h):
        return 4 if d == h else 3

    HB = FB // 2

    def act_part(n, h):
        return actt.at[zrel(n), pl.ds(h * HB, HB)]

    def act_send(s):
        for h_ in (0, 1):
            for d in (0, 1):
                h = h_ ^ d
                if s <= hops(d, h):
                    p = act_part((1 - s) if d == 0 else (s - 1), h)
                    remote(p, p, act_s.at[d, s - 1, h], act_r.at[d, s - 1, h], zdev(d)).start()

    def act_take(s):
        for h_ in (0, 1):
            for d in (0, 1):
                h = h_ ^ d
                if s <= hops(d, h):
                    p = act_part(-s if d == 0 else s, h)
                    remote(p, p, act_s.at[d, s - 1, h], act_r.at[d, s - 1, h], zdev(d)).wait_recv()
                    if s + 1 <= hops(d, h):
                        remote(p, p, act_s.at[d, s, h], act_r.at[d, s, h], zdev(d)).start()

    locals_[1].wait()
    locals_[2].wait()
    for q in range(FB // 128):
        cols = pl.ds(q * 128, 128)
        g = gv[:, cols].astype(F32)
        a = (g * jax.nn.sigmoid(g) * uv[:, cols].astype(F32)).astype(BF)
        actt[z, cols, :] = a.astype(F32).T.astype(BF)
    act_send(1)

    pass_on(1, 8, *ogx)
    act_take(1)
    pass_on(8, NCHIP, *ogx)
    wait_shared(og, ogc_s, ogc_r)
    locals_[3].wait()
    send_own(*xx)

    def rows(b):
        return pl.ds(pl.multiple_of(b * TB, TB), TB)

    def make_terms(rels):
        a = jnp.concatenate([og[rows(zrel(r)), :] for r in rels], axis=0) if len(rels) > 1 else og[rows(zrel(rels[0])), :]

        def body(i, _):
            lanes = pl.ds(pl.multiple_of(i * 128, 128), 128)
            t = nt(a, wd[lanes, :])
            for n, r in enumerate(rels):
                terms[r, :, lanes] = t[n * TB : (n + 1) * TB].astype(BF).astype(F32)
            return 0

        lax.fori_loop(0, FB // 128, body, 0)

    def half(h):
        return pl.ds(h * (TB // 2), TB // 2)

    def rs_copy(d, s, h):
        return remote(
            rs_out.at[d, s - 1, half(h)], rs_in.at[d, s - 1, half(h)],
            rs_s.at[d, s - 1, h], rs_r.at[d, s - 1, h], zdev(d),
        )

    def rs_step(s, fresh):
        for h_ in (0, 1):
            for d in (0, 1):
                h = h_ ^ d
                first = 1 if h == d else 2
                if s < first or (s == first) != fresh:
                    continue
                t = terms[5 - s if d == 0 else 3 + s, half(h), :]
                if not fresh:
                    rs_copy(d, s - 1, h).wait_recv()
                    t = t + rs_in[d, s - 2, half(h), :].astype(F32)
                rs_out[d, s - 1, half(h), :] = t.astype(BF)
                rs_copy(d, s, h).start()

    locals_[4].wait()
    make_terms([4])
    rs_step(1, True)
    make_terms([3, 5])
    rs_step(2, True)
    act_take(2)
    rs_step(2, False)
    make_terms([2, 6])
    act_take(3)
    rs_step(3, False)
    make_terms([1, 7])
    make_terms([0])
    pass_on(1, 8, *xx)
    rs_step(4, False)
    act_take(4)
    pass_on(8, NCHIP, *xx)

    for d in (0, 1):
        for h in (0, 1):
            rs_copy(d, 4, h).wait_recv()
    for q in range(FB // 128):
        cols = pl.ds(q * 128, 128)
        g, u = gv[:, cols].astype(F32), uv[:, cols].astype(F32)
        up = terms[0, :, cols] + rs_in[0, 3, :, cols].astype(F32) + rs_in[1, 3, :, cols].astype(F32)
        s = jax.nn.sigmoid(g)
        dl[z, 0, :, cols] = (up * u * s * (1.0 + g * (1.0 - s))).astype(BF)
        dl[z, 1, :, cols] = (up * (g * s)).astype(BF)

    def ag_copy(d, s, a):
        p = dl.at[zrel((1 - s) if d == 0 else (s - 1)), a]
        return remote(p, p, ag_s.at[d, s - 1, a], ag_r.at[d, s - 1, a], zdev(d))

    def ag_take(s):
        for a_ in (0, 1):
            for d in (0, 1):
                a = a_ ^ d
                if s <= hops(d, a):
                    p = dl.at[zrel(-s if d == 0 else s), a]
                    remote(p, p, ag_s.at[d, s - 1, a], ag_r.at[d, s - 1, a], zdev(d)).wait_recv()
                    if s + 1 <= hops(d, a):
                        ag_copy(d, s + 1, a).start()

    for a_ in (0, 1):
        for d in (0, 1):
            ag_copy(d, 1, a_ ^ d).start()

    def down(i, _):
        r = pl.ds(pl.multiple_of(i * 128, 128), 128)
        a = jnp.concatenate([actt[b, r, :] for b in range(NZ)], axis=1)
        gdn[r, :] = nn(a, og[...]).astype(BF)
        return 0

    lax.fori_loop(0, FB // 128, down, 0)
    out_down = pltpu.make_async_copy(gdn, gdn_h, outs.at[0])
    out_down.start()

    wait_shared(xa, xc_s, xc_r)

    def flip(b, _):
        for q in range(DB // 128):
            v = xa[rows(b), pl.ds(q * 128, 128)].astype(F32)
            xt[b, pl.ds(q * 128, 128), :] = v.T.astype(BF)
        return 0

    lax.fori_loop(0, NZ, flip, 0)
    locals_[5].wait()
    locals_[6].wait()

    def grads(blocks, first, last):
        def cat(vals, axis):
            return vals[0] if len(vals) == 1 else jnp.concatenate(vals, axis=axis)

        def body(i, _):
            r = pl.ds(pl.multiple_of(i * 256, 256), 256)
            xb = cat([xt[b, r, :] for b in blocks], 1)
            for a in (0, 1):
                t = nn(xb, cat([dl[b, a] for b in blocks], 0))
                if not first:
                    t = t + acc[a, r, :]
                if last:
                    stage[a, r, :] = t.astype(BF)
                else:
                    acc[a, r, :] = t
            return 0

        lax.fori_loop(0, DB // 256, body, 0)

    def core_copy(c):
        return remote(cs.at[c], cr.at[c], cs_s.at[c], cs_r.at[c], sib)

    def inputs(blocks):
        gdb = jnp.concatenate([dl[b, 0] for b in blocks], axis=0) if len(blocks) > 1 else dl[blocks[0], 0]
        udb = jnp.concatenate([dl[b, 1] for b in blocks], axis=0) if len(blocks) > 1 else dl[blocks[0], 1]

        def body(i, _):
            n = pl.ds(pl.multiple_of(i * 256, 256), 256)
            t = nt(gdb, wg[n, :]) + nt(udb, wu[n, :])
            for m, b in enumerate(blocks):
                for e in (0, 1):
                    base = m * TB + e * 2 * PR
                    lo, hi = t[base : base + PR], t[base + PR : base + 2 * PR]
                    own[2 * b + e, :, n] = jnp.where(core == 0, lo, hi)
                    cs[2 * b + e, :, n] = jnp.where(core == 0, hi, lo).astype(BF)
            return 0

        lax.fori_loop(0, DB // 256, body, 0)
        for b in blocks:
            for e in (0, 1):
                core_copy(2 * b + e).start()

    def reduce_copy(c):
        j = lax.rem(c - chip + NCHIP, NCHIP)
        return remote(sx.at[c], rr.at[j], rr_s.at[j], rr_r.at[j], (z, 2 * c + core))

    def push(blocks):
        for b in blocks:
            for e in (0, 1):
                c = 2 * b + e
                core_copy(c).wait_recv()
                t = own[c] + cr[c].astype(F32)
                own[c] = t
                sx[c] = t.astype(BF)

                @pl.when(c != chip)
                def _():
                    reduce_copy(c).start()

    pending = [z]
    inputs(pending)
    grads(pending, True, False)
    for s in (1, 2, 3):
        ag_take(s)
        push(pending)
        pending = [zrel(-s), zrel(s)]
        inputs(pending)
        grads(pending, False, False)
    push(pending)
    ag_take(4)
    pending = [zrel(4)]
    inputs(pending)
    push(pending)
    grads(pending, False, True)
    out_gate = pltpu.make_async_copy(stage.at[0], gg_h, outs.at[1])
    out_up = pltpu.make_async_copy(stage.at[1], gu_h, outs.at[2])
    out_gate.start()
    out_up.start()

    def arrive(j, _):
        remote(sx.at[0], rr.at[j], rr_s.at[j], rr_r.at[j], sib).wait_recv()
        return 0

    lax.fori_loop(1, NCHIP, arrive, 0)
    total = own[chip]
    for j in range(1, NCHIP):
        total = total + rr[j].astype(F32)
    gi[...] = total.astype(BF)
    out_gi = pltpu.make_async_copy(gi, gi_h, outs.at[3])
    out_gi.start()

    def gone(j, _):
        spread(og, j, og_s, og_r).wait_send()
        spread(xa, j, x_s, x_r).wait_send()
        remote(sx.at[0], rr.at[j], rr_s.at[j], rr_r.at[j], sib).wait_send()
        return 0

    lax.fori_loop(1, NCHIP, gone, 0)

    def gone_core(j, _):
        share(og, j, ogc_s, ogc_r).wait_send()
        share(xa, j, xc_s, xc_r).wait_send()
        core_copy(j).wait_send()
        return 0

    lax.fori_loop(0, NCHIP, gone_core, 0)
    for d in (0, 1):
        for h in (0, 1):
            for s in range(1, 5):
                if s <= hops(d, h):
                    p = act_part(0, h)
                    remote(p, p, act_s.at[d, s - 1, h], act_r.at[d, s - 1, h], zdev(d)).wait_send()
                    ag_copy(d, s, h).wait_send()
                if s >= (1 if h == d else 2):
                    rs_copy(d, s, h).wait_send()
    out_down.wait()
    out_gate.wait()
    out_up.wait()
    out_gi.wait()


def on_device(block_input, output_grad, gate_pre, up_pre, w_gate, w_up, w_down):
    dma = pltpu.SemaphoreType.DMA
    any_ = pl.BlockSpec(memory_space=pl.ANY)
    ring = [dma((2, 4, 2))] * 2
    plane = [dma((NCHIP,))] * 2
    return pl.pallas_call(
        kernel,
        out_shape=(
            jax.ShapeDtypeStruct((PR, DB), BF),
            jax.ShapeDtypeStruct((DB, FB), BF),
            jax.ShapeDtypeStruct((DB, FB), BF),
            jax.ShapeDtypeStruct((FB, DB), BF),
        ),
        in_specs=[any_] * 7,
        out_specs=(any_,) * 4,
        scratch_shapes=[
            pltpu.VMEM((1024, DB), BF),
            pltpu.VMEM((1024, DB), BF),
            pltpu.VMEM((NZ, DB, TB), BF),
            pltpu.VMEM((TB, FB), BF),
            pltpu.VMEM((TB, FB), BF),
            pltpu.VMEM((DB, FB), BF),
            pltpu.VMEM((DB, FB), BF),
            pltpu.VMEM((FB, DB), BF),
            pltpu.VMEM((NZ, FB, TB), BF),
            pltpu.VMEM((NZ, 2, TB, FB), BF),
            pltpu.VMEM((NZ, TB, FB), F32),
            pltpu.VMEM((2, 4, TB, FB), BF),
            pltpu.VMEM((2, 4, TB, FB), BF),
            pltpu.VMEM((2, DB, FB), F32),
            pltpu.VMEM((2, DB, FB), BF),
            pltpu.VMEM((FB, DB), BF),
            pltpu.VMEM((NCHIP, PR, DB), F32),
            pltpu.VMEM((NCHIP, PR, DB), BF),
            pltpu.VMEM((NCHIP, PR, DB), BF),
            pltpu.VMEM((NCHIP, PR, DB), BF),
            pltpu.VMEM((NCHIP, PR, DB), BF),
            pltpu.VMEM((PR, DB), BF),
            dma((7,)),
            *ring,
            *plane, *plane,
            *plane, *plane,
            *ring,
            *ring,
            *plane,
            *plane,
            dma((4,)),
        ],
        compiler_params=pltpu.CompilerParams(
            collective_id=0, has_side_effects=True, vmem_limit_bytes=56 * 2**20
        ),
        name="ffn_grad",
    )(block_input, output_grad, gate_pre, up_pre, w_gate, w_up, w_down)


def solution(mesh):
    return jax.shard_map(
        on_device,
        mesh=mesh,
        in_specs=(
            P("col", "row"),
            P("col", "row"),
            P("row", "col"),
            P("row", "col"),
            P("row", "col"),
            P("row", "col"),
            P("col", "row"),
        ),
        out_specs=(P("col", "row"), P("row", "col"), P("row", "col"), P("col", "row")),
        check_vma=False,
    )
```

time: 380 us -> 121 us (0.32)
  waiting for transfers between devices: 320 us -> 0 us
  Pallas kernels: 0 us -> 112 us
  matrix products: 35 us -> 0 us
  between operations: 14.1 us -> 0.64 us
    all_gather x5 -> x0, waiting for transfers between devices: 193 us -> none  [the longest x1 53.9 us: on_device(): lax.all_gather(output_grad, 'col', axis=0, tiled=True)]
    reduce_scatter x2 -> x0, waiting for transfers between devices: 125 us -> none  [the longest x1 83.6 us: on_device(): lax.psum_scatter(input_part.astype(jnp.bfloat16), 'col', scatter_dimensio...]
    pallas_call x0 -> x1, Pallas kernels: none -> 112 us  [on_device(): pl.pallas_call(kernel, out_shape=(jax.ShapeDtypeStruct((PR, DB), BF), jax...]
    dot_general x6 -> x0, matrix products: 35 us -> none  [the longest x3 18.6 us: contract_cols(): lax.dot_general(left, right, (((1,), (1,)), ((), ())), preferred_element_...]
  transfers between devices with their start and end apart: 7 -> 0, of which waited for: 7 -> 0; matrix products, arithmetic and copies ran while one was open for 10% -> 0% of each run, Pallas kernels for 0% -> 0%
where the time goes in v1:
time: 121 us; the launch traced here: 120 us
  Pallas kernels  112 us (93%)
  local copies, waits for them, and re-layouts  7.87 us (7%)
    pallas_call x1, Pallas kernels, on_device(): pl.pallas_call(kernel, out_shape=(jax.ShapeDtypeStruct((PR, DB), BF), jax...  112 us
    unnamed x8, local copies, waits for them, and re-layouts  7.87 us

profile of v1, /device:TPU:4, one launch (start us, length us, event | category | flops | bytes accessed | tf_op | source)
XLA Modules:
  0.0 120.3 jit_solution(4615597843081320233)
XLA Ops:
  0.6 111.8 %ffn_grad.1 = (bf16[32,1024]{1,0:T(8,128)(2,1)}, bf16[1024,896]{1,0:T(8,128)(2,1)}, bf16[1024,896]{1,0:T(8,128)(2,1)}, bf16[896,1024]{1,0:T(8,128)(2,1)}) custom-call(bf16[32,1024]{1,0:T(8,128)(2,1)} %x_h.1, bf16[32,1024]{1,0:T(8,128)(2,1)} %og_h.1, bf16[128,896]{1,0:T(8,128)(2,1)} %g_h.1, bf16[128,896]{1,0:T(8,128)(2,1)} %u_h.1, bf16[1024,896]{1,0:T(8,128)(2,1)} %wg_h.1, ...), custom_call_target="tpu_custom_call" | custom-call | tf_op jit(solution)/shard_map/ffn_grad/pallas_call | solution.py:399
  112.4 1.5 %copy.15 = bf16[32,1024]{1,0:T(8,128)(2,1)} copy(bf16[32,1024]{1,0:T(8,128)(2,1)} %get-tuple-element.8) | data formatting | bytes 131072
  113.9 0.0 copy-start.1
  113.9 3.0 %copy.16 = bf16[1024,896]{1,0:T(8,128)(2,1)} copy(bf16[1024,896]{1,0:T(8,128)(2,1)} %get-tuple-element.9) | data formatting | bytes 3670016
  116.9 0.0 copy-done.1
  116.9 0.0 copy-start
  116.9 1.2 %copy.17 = bf16[1024,896]{1,0:T(8,128)(2,1)} copy(bf16[1024,896]{1,0:T(8,128)(2,1)S(1)} %copy-done.1) | data formatting | bytes 3670016
  118.1 0.9 copy-done
  119.1 1.2 %copy.18 = bf16[896,1024]{1,0:T(8,128)(2,1)} copy(bf16[896,1024]{1,0:T(8,128)(2,1)S(1)} %copy-done) | data formatting | bytes 3670016
Async XLA Ops:
  113.9 3.0 %copy-start.1 = (bf16[1024,896]{1,0:T(8,128)(2,1)S(1)}, bf16[1024,896]{1,0:T(8,128)(2,1)}, u32[]{:S(2)}) copy-start(bf16[1024,896]{1,0:T(8,128)(2,1)} %get-tuple-element.10) | copy-start | bytes 5505028
  116.9 2.2 %copy-start = (bf16[896,1024]{1,0:T(8,128)(2,1)S(1)}, bf16[896,1024]{1,0:T(8,128)(2,1)}, u32[]{:S(2)}) copy-start(bf16[896,1024]{1,0:T(8,128)(2,1)} %get-tuple-element.11) | copy-start | bytes 5505028

commit v2 on v1

v2 whole, which is shorter than its diff:
```python
import functools

import jax
import jax.numpy as jnp
from jax import lax
from jax.experimental import pallas as pl
from jax.experimental.pallas import tpu as pltpu
from jax.sharding import PartitionSpec as P

MESH = pl.DeviceIdType.MESH
BF, F32 = jnp.bfloat16, jnp.float32
NZ, NCHIP = 8, 16
TB = 128
HT = 64
DB = 1024
FB = 896
PR = 32


def nt(a, b):
    return lax.dot_general(a, b, (((1,), (1,)), ((), ())), preferred_element_type=F32)


def nn(a, b):
    return lax.dot_general(a, b, (((1,), (0,)), ((), ())), preferred_element_type=F32)


def kernel(
    x_h, og_h, g_h, u_h, wg_h, wu_h, wd_h,
    gi, stage_g, stage_u, gdn,
    og, xa, xt, gu, gl, wg, wu, wd, act, up, dl, terms, rs_out, rs_in, acc, own, cs, cr, s1, r1, s2, rr,
    loc, ring_s, ring_r, og_s, og_r, ogc_s, ogc_r, x_s, x_r, xc_s, xc_r, rs_s, rs_r, cs_s, cs_r, p1_s, p1_r, rr_s, rr_r,
):
    z, col = lax.axis_index("row"), lax.axis_index("col")
    chip, core = col // 2, lax.rem(col, 2)
    cx = chip // 4
    sib = (z, col + 1 - 2 * core)

    def zdev(d):
        return (lax.rem(z + (1 if d == 0 else NZ - 1), NZ), col)

    def zrel(n):
        return lax.rem(z + (n % NZ), NZ)

    def chip_at(j):
        return lax.rem(chip + j + NCHIP, NCHIP)

    def chip_dev(j):
        return (z, 2 * chip_at(j) + core)

    def remote(src, dst, ss, rs, dev):
        return pltpu.make_async_remote_copy(
            src_ref=src, dst_ref=dst, send_sem=ss, recv_sem=rs, device_id=dev, device_id_type=MESH
        )

    mine = pl.ds(pl.multiple_of(col * PR, PR), PR)
    locals_ = [
        pltpu.make_async_copy(g_h.at[pl.ds(0, HT)], gu.at[z, 0], loc.at[0]),
        pltpu.make_async_copy(u_h.at[pl.ds(0, HT)], gu.at[z, 1], loc.at[1]),
        pltpu.make_async_copy(og_h, og.at[mine], loc.at[2]),
        pltpu.make_async_copy(g_h.at[pl.ds(HT, HT)], gl.at[0], loc.at[3]),
        pltpu.make_async_copy(u_h.at[pl.ds(HT, HT)], gl.at[1], loc.at[4]),
        pltpu.make_async_copy(x_h, xa.at[mine], loc.at[5]),
        pltpu.make_async_copy(wd_h, wd, loc.at[6]),
        pltpu.make_async_copy(wg_h, wg, loc.at[7]),
        pltpu.make_async_copy(wu_h, wu, loc.at[8]),
    ]
    for c in locals_:
        c.start()

    bar = pltpu.get_barrier_semaphore()
    for d in (0, 1):
        pl.semaphore_signal(bar, inc=1, device_id=zdev(d), device_id_type=MESH)
    pl.semaphore_signal(bar, inc=1, device_id=sib, device_id_type=MESH)

    def greet(j, _):
        pl.semaphore_signal(bar, inc=1, device_id=chip_dev(j), device_id_type=MESH)
        return 0

    lax.fori_loop(1, NCHIP, greet, 0)
    pl.semaphore_wait(bar, NCHIP + 2)

    def piece(buf, j):
        return buf.at[pl.ds(pl.multiple_of((2 * chip_at(j) + core) * PR, PR), PR)]

    def spread(buf, j, ss, rs):
        return remote(buf.at[mine], buf.at[mine], ss.at[j], rs.at[j], chip_dev(j))

    def landed(buf, j, ss, rs):
        p = piece(buf, NCHIP - j)
        return remote(p, p, ss.at[j], rs.at[j], chip_dev(j))

    def share(buf, j, ss, rs):
        p = piece(buf, NCHIP - j)
        return remote(p, p, ss.at[j], rs.at[j], sib)

    def shared(buf, j, ss, rs):
        p = buf.at[pl.ds(pl.multiple_of((2 * chip_at(NCHIP - j) + 1 - core) * PR, PR), PR)]
        return remote(p, p, ss.at[j], rs.at[j], sib)

    def send_own(buf, s, r, cs_, cr_):
        def body(j, _):
            spread(buf, j, s, r).start()
            return 0

        lax.fori_loop(1, NCHIP, body, 0)
        share(buf, 0, cs_, cr_).start()

    def pass_on(lo, hi, buf, s, r, cs_, cr_):
        def body(j, _):
            landed(buf, j, s, r).wait_recv()
            share(buf, j, cs_, cr_).start()
            return 0

        lax.fori_loop(lo, hi, body, 0)

    def wait_shared(buf, cs_, cr_):
        def body(j, _):
            shared(buf, j, cs_, cr_).wait_recv()
            return 0

        lax.fori_loop(0, NCHIP, body, 0)

    ogx, xx = (og, og_s, og_r, ogc_s, ogc_r), (xa, x_s, x_r, xc_s, xc_r)

    G, U, UP, GD, UD, ACT = range(6)
    low, high = pl.ds(0, HT), pl.ds(HT, HT)

    def ring_ref(i, n):
        b = zrel(n)
        return (
            lambda: gu.at[b, 0],
            lambda: gu.at[b, 1],
            lambda: up.at[b],
            lambda: dl.at[b, 0, high],
            lambda: dl.at[b, 1, high],
            lambda: act.at[b, high],
        )[i]()

    LONG = (0, 1, 1, 0, 1, 0)

    def hops(d, i):
        return 4 if LONG[i] == d else 3

    def ring_copy(i, d, s, n):
        p = ring_ref(i, n)
        return remote(p, p, ring_s.at[i, d, s - 1], ring_r.at[i, d, s - 1], zdev(d))

    def ring_send(i):
        for d in (LONG[i], 1 - LONG[i]):
            ring_copy(i, d, 1, 0).start()

    def ring_take(i, s):
        for d in (LONG[i], 1 - LONG[i]):
            if s <= hops(d, i):
                n = -s if d == 0 else s
                ring_copy(i, d, s, n).wait_recv()
                if s + 1 <= hops(d, i):
                    ring_copy(i, d, s + 1, n).start()

    locals_[0].wait()
    ring_send(G)
    locals_[1].wait()
    ring_send(U)
    locals_[2].wait()
    send_own(*ogx)

    def silu_parts(g, u):
        s = jax.nn.sigmoid(g)
        return g * s, u * s * (1.0 + g * (1.0 - s))

    def tiles(body):
        def step(q, _):
            body(pl.ds(pl.multiple_of(q * 128, 128), 128))
            return 0

        lax.fori_loop(0, FB // 128, step, 0)

    locals_[3].wait()
    locals_[4].wait()

    def own_act(cols):
        g, u = gl[0, :, cols].astype(F32), gl[1, :, cols].astype(F32)
        act[z, high, cols] = (g * jax.nn.sigmoid(g) * u).astype(BF)

    tiles(own_act)

    ring_send(ACT)
    ring_take(G, 1)
    ring_take(U, 1)
    pass_on(1, 4, *ogx)
    ring_take(ACT, 1)
    pass_on(4, 10, *ogx)
    ring_take(G, 2)
    pass_on(10, NCHIP, *ogx)
    ring_take(U, 2)
    wait_shared(og, ogc_s, ogc_r)

    def rows(b):
        return pl.ds(pl.multiple_of(b * TB, TB), TB)

    def make_terms(rels):
        a = jnp.concatenate([og[rows(zrel(r)), :] for r in rels], axis=0) if len(rels) > 1 else og[rows(zrel(rels[0])), :]

        def tile(lanes):
            t = nt(a, wd[lanes, :])
            for n, r in enumerate(rels):
                terms[r, :, lanes] = t[n * TB : (n + 1) * TB].astype(BF).astype(F32)

        def body(i, _):
            tile(pl.ds(pl.multiple_of(i * 256, 256), 256))
            return 0

        lax.fori_loop(0, 3, body, 0)
        tile(pl.ds(768, 128))

    QT = TB // 4

    def rs_copy(d, s, q):
        r = pl.ds(q * QT, QT)
        return remote(
            rs_out.at[d, s - 1, r], rs_in.at[d, s - 1, r], rs_s.at[d, s - 1, q], rs_r.at[d, s - 1, q], zdev(d)
        )

    def rs_step(s, fresh):
        for o in (2, 3, 0, 1):
            for d in (0, 1):
                q = o ^ (2 * d)
                first = 1 if o < 2 else 2
                if s < first or (s == first) != fresh:
                    continue
                r = pl.ds(q * QT, QT)
                t = terms[5 - s if d == 0 else 3 + s, r, :]
                if not fresh:
                    rs_copy(d, s - 1, q).wait_recv()
                    t = t + rs_in[d, s - 2, r, :].astype(F32)
                rs_out[d, s - 1, r, :] = t.astype(BF)
                rs_copy(d, s, q).start()

    def all_act(lo, hi):
        def block(b, _):
            def body(cols):
                g, u = gu[b, 0, :, cols].astype(F32), gu[b, 1, :, cols].astype(F32)
                act[b, low, cols] = (g * jax.nn.sigmoid(g) * u).astype(BF)

            tiles(body)
            return 0

        lax.fori_loop(lo, hi, block, 0)

    def down(lo, hi, width):
        def body(i, _):
            cols = pl.ds(pl.multiple_of(i * width, width), width)
            a = jnp.concatenate([act[b, :, cols] for b in range(NZ)], axis=0)
            gdn[cols, :] = nn(a.astype(F32).T.astype(BF), og[...]).astype(BF)
            return 0

        lax.fori_loop(lo, hi, body, 0)

    def flip(b, _):
        for q in range(DB // 128):
            v = xa[rows(b), pl.ds(q * 128, 128)].astype(F32)
            xt[b, pl.ds(q * 128, 128), :] = v.T.astype(BF)
        return 0

    locals_[6].wait()
    make_terms([4])
    rs_step(1, True)
    make_terms([3, 5, 2, 6])
    rs_step(2, True)
    ring_take(G, 3)
    locals_[5].wait()
    send_own(*xx)
    rs_step(2, False)
    ring_take(U, 3)
    make_terms([1, 7, 0])
    rs_step(3, False)
    ring_take(G, 4)
    ring_take(U, 4)
    rs_step(4, False)
    ring_take(ACT, 2)
    pass_on(1, NCHIP, *xx)
    all_act(0, 8)

    for d in (0, 1):
        for q in (0, 1):
            rs_copy(d, 4, q).wait_recv()

    def own_up(cols):
        t = terms[0, low, cols] + rs_in[0, 3, low, cols].astype(F32) + rs_in[1, 3, low, cols].astype(F32)
        up[z, :, cols] = t.astype(BF)

    tiles(own_up)
    ring_send(UP)
    for d in (0, 1):
        for q in (2, 3):
            rs_copy(d, 4, q).wait_recv()

    def own_deltas(cols):
        t = terms[0, high, cols] + rs_in[0, 3, high, cols].astype(F32) + rs_in[1, 3, high, cols].astype(F32)
        su, sg = silu_parts(gl[0, :, cols].astype(F32), gl[1, :, cols].astype(F32))
        dl[z, 0, high, cols] = (t * sg).astype(BF)
        dl[z, 1, high, cols] = (t * su).astype(BF)

    tiles(own_deltas)
    ring_send(GD)
    ring_send(UD)

    def deltas(blocks):
        for b in blocks:

            def body(cols, b=b):
                su, sg = silu_parts(gu[b, 0, :, cols].astype(F32), gu[b, 1, :, cols].astype(F32))
                t = up[b, :, cols].astype(F32)
                dl[b, 0, low, cols] = (t * sg).astype(BF)
                dl[b, 1, low, cols] = (t * su).astype(BF)

            tiles(body)

    wait_shared(xa, xc_s, xc_r)
    lax.fori_loop(0, NZ, flip, 0)
    locals_[7].wait()
    locals_[8].wait()

    def grads(blocks, first, last):
        def cat(vals, axis):
            return vals[0] if len(vals) == 1 else jnp.concatenate(vals, axis=axis)

        def body(i, _):
            r = pl.ds(pl.multiple_of(i * 512, 512), 512)
            xb = cat([xt[b, r, :] for b in blocks], 1)
            for a in (0, 1):
                t = nn(xb, cat([dl[b, a] for b in blocks], 0))
                if not first:
                    t = t + acc[a, r, :]
                if last:
                    (stage_g, stage_u)[a][r, :] = t.astype(BF)
                else:
                    acc[a, r, :] = t
            return 0

        lax.fori_loop(0, DB // 512, body, 0)

    def core_copy(b):
        return remote(cs.at[b], cr.at[b], cs_s.at[b], cs_r.at[b], sib)

    def x_copy(b, dx):
        return remote(s1.at[b, dx], r1.at[b, dx], p1_s.at[b, dx], p1_r.at[b, dx], chip_dev(4 * dx))

    def inputs(blocks):
        gdb = jnp.concatenate([dl[b, 0] for b in blocks], axis=0) if len(blocks) > 1 else dl[blocks[0], 0]
        udb = jnp.concatenate([dl[b, 1] for b in blocks], axis=0) if len(blocks) > 1 else dl[blocks[0], 1]

        def body(i, _):
            n = pl.ds(pl.multiple_of(i * 256, 256), 256)
            t = nt(gdb, wg[n, :]) + nt(udb, wu[n, :])
            for m, b in enumerate(blocks):
                for e in (0, 1):
                    base = m * TB + e * 2 * PR
                    lo, hi = t[base : base + PR], t[base + PR : base + 2 * PR]
                    own[b, i, pl.ds(e * PR, PR), :] = jnp.where(core == 0, lo, hi)
                    cs[b, i, pl.ds(e * PR, PR), :] = jnp.where(core == 0, hi, lo).astype(BF)
            return 0

        lax.fori_loop(0, DB // 256, body, 0)
        for b in blocks:
            core_copy(b).start()

    def sum_cores(blocks):
        for b in blocks:
            core_copy(b).wait_recv()
            for dx in (1, 2, 3, 0):
                i = lax.rem(cx + dx, 4)
                t = own[b, i] + cr[b, i].astype(F32)
                if dx == 0:
                    own[b, i] = t
                else:
                    s1[b, dx] = t.astype(BF)
                    x_copy(b, dx).start()

    def reduce_copy(b, e, j):
        return remote(
            s2.at[b, pl.ds(e * PR, PR)], rr.at[j], rr_s.at[j], rr_r.at[j], (z, 2 * (2 * b + e) + core)
        )

    def sum_x(blocks):
        for b in blocks:
            t = own[b, cx]
            for dx in (1, 2, 3):
                x_copy(b, dx).wait_recv()
                t = t + r1[b, dx].astype(F32)
            own[b, cx] = t
            s2[b] = t.astype(BF)
            for e in (0, 1):
                c = 2 * b + e

                @pl.when(c != chip)
                def _(b=b, e=e, c=c):
                    reduce_copy(b, e, lax.rem(c - chip + NCHIP, NCHIP)).start()

    def step_blocks(s):
        return [z] if s == 0 else [zrel(4)] if s == 4 else [zrel(-s), zrel(s)]

    deltas(step_blocks(0))
    inputs(step_blocks(0))
    ring_take(UP, 1)
    grads(step_blocks(0), True, False)
    ring_take(GD, 1)
    sum_cores(step_blocks(0))
    ring_take(UD, 1)
    for s in (1, 2, 3):
        now, before = step_blocks(s), step_blocks(s - 1)
        deltas(now)
        inputs(now)
        ring_take(UP, s + 1)
        grads(now, False, False)
        ring_take(GD, s + 1)
        sum_x(before)
        sum_cores(now)
        ring_take(UD, s + 1)
        if s == 2:
            ring_take(ACT, 3)
    now = step_blocks(4)
    deltas(now)
    inputs(now)
    sum_x(step_blocks(3))
    sum_cores(now)
    grads(now, False, True)
    sum_x(now)
    ring_take(ACT, 4)
    down(0, 3, 256)
    down(6, 7, 128)

    def arrive(j, _):
        remote(s2.at[0, pl.ds(0, PR)], rr.at[j], rr_s.at[j], rr_r.at[j], sib).wait_recv()
        return 0

    lax.fori_loop(1, NCHIP, arrive, 0)
    rr[0] = own[chip // 2, cx, pl.ds(pl.multiple_of(lax.rem(chip, 2) * PR, PR), PR), :].astype(BF)
    for q in range(4):
        t = jnp.zeros((PR, 256), F32)
        for yy in range(4):
            t = t + rr[lax.rem(chip - (4 * q + yy) + NCHIP, NCHIP)].astype(F32)
        gi[:, q * 256 : (q + 1) * 256] = t.astype(BF)

    def gone(j, _):
        spread(og, j, og_s, og_r).wait_send()
        spread(xa, j, x_s, x_r).wait_send()
        remote(s2.at[0, pl.ds(0, PR)], rr.at[j], rr_s.at[j], rr_r.at[j], sib).wait_send()
        return 0

    lax.fori_loop(1, NCHIP, gone, 0)

    def gone_core(j, _):
        share(og, j, ogc_s, ogc_r).wait_send()
        share(xa, j, xc_s, xc_r).wait_send()
        return 0

    lax.fori_loop(0, NCHIP, gone_core, 0)

    def gone_block(b, _):
        core_copy(b).wait_send()
        for dx in (1, 2, 3):
            x_copy(b, dx).wait_send()
        return 0

    lax.fori_loop(0, NZ, gone_block, 0)
    for d in (0, 1):
        for i in range(6):
            for s in range(1, hops(d, i) + 1):
                ring_copy(i, d, s, 0).wait_send()
        for q in range(4):
            for s in range(1 if q // 2 == d else 2, 5):
                rs_copy(d, s, q).wait_send()


def write_out(*refs):
    sems = refs[8]
    copies = [pltpu.make_async_copy(refs[i], refs[4 + i], sems.at[i]) for i in range(4)]
    for c in copies:
        c.start()
    for c in copies:
        c.wait()


def on_device(block_input, output_grad, gate_pre, up_pre, w_gate, w_up, w_down):
    dma = pltpu.SemaphoreType.DMA
    any_ = pl.BlockSpec(memory_space=pl.ANY)
    plane = [dma((NCHIP,))] * 2
    shapes = ((PR, DB), (DB, FB), (DB, FB), (FB, DB))
    vmem = pl.BlockSpec(memory_space=pltpu.VMEM)
    held = pl.pallas_call(
        kernel,
        out_shape=tuple(pltpu.VMEM(s, BF) for s in shapes),
        in_specs=[any_] * 7,
        out_specs=(vmem,) * 4,
        scratch_shapes=[
            pltpu.VMEM((1024, DB), BF),
            pltpu.VMEM((1024, DB), BF),
            pltpu.VMEM((NZ, DB, TB), BF),
            pltpu.VMEM((NZ, 2, HT, FB), BF),
            pltpu.VMEM((2, HT, FB), BF),
            pltpu.VMEM((DB, FB), BF),
            pltpu.VMEM((DB, FB), BF),
            pltpu.VMEM((FB, DB), BF),
            pltpu.VMEM((NZ, TB, FB), BF),
            pltpu.VMEM((NZ, HT, FB), BF),
            pltpu.VMEM((NZ, 2, TB, FB), BF),
            pltpu.VMEM((NZ, TB, FB), F32),
            pltpu.VMEM((2, 4, TB, FB), BF),
            pltpu.VMEM((2, 4, TB, FB), BF),
            pltpu.VMEM((2, DB, FB), F32),
            pltpu.VMEM((NZ, 4, 2 * PR, 256), F32),
            pltpu.VMEM((NZ, 4, 2 * PR, 256), BF),
            pltpu.VMEM((NZ, 4, 2 * PR, 256), BF),
            pltpu.VMEM((NZ, 4, 2 * PR, 256), BF),
            pltpu.VMEM((NZ, 4, 2 * PR, 256), BF),
            pltpu.VMEM((NZ, 2 * PR, 256), BF),
            pltpu.VMEM((NCHIP, PR, 256), BF),
            dma((9,)),
            *[dma((6, 2, 4))] * 2,
            *plane, *plane,
            *plane, *plane,
            *[dma((2, 4, 4))] * 2,
            *[dma((NZ,))] * 2,
            *[dma((NZ, 4))] * 2,
            *plane,
        ],
        compiler_params=pltpu.CompilerParams(
            collective_id=0, has_side_effects=True, vmem_limit_bytes=56 * 2**20
        ),
        name="ffn_grad",
    )(block_input, output_grad, gate_pre, up_pre, w_gate, w_up, w_down)
    return pl.pallas_call(
        write_out,
        out_shape=tuple(jax.ShapeDtypeStruct(s, BF) for s in shapes),
        in_specs=[vmem] * 4,
        out_specs=(any_,) * 4,
        scratch_shapes=[dma((4,))],
        compiler_params=pltpu.CompilerParams(vmem_limit_bytes=2**20),
        name="write_out",
    )(*held)


def solution(mesh):
    return jax.shard_map(
        on_device,
        mesh=mesh,
        in_specs=(
            P("col", "row"),
            P("col", "row"),
            P("row", "col"),
            P("row", "col"),
            P("row", "col"),
            P("row", "col"),
            P("col", "row"),
        ),
        out_specs=(P("col", "row"), P("row", "col"), P("row", "col"), P("col", "row")),
        check_vma=False,
    )
```

time: 121 us -> 104 us (0.86)
  Pallas kernels: 112 us -> 103 us
  local copies, waits for them, and re-layouts: 7.87 us -> 0 us
    pallas_call x1 -> x2, Pallas kernels: 112 us -> 103 us  [the longest x1 101 us: on_device(): pl.pallas_call(kernel, out_shape=tuple((pltpu.VMEM(s, BF) for s in shapes...]
    unnamed x8 -> x0, local copies, waits for them, and re-layouts: 7.87 us -> none
where the time goes in v2:
time: 104 us
  Pallas kernels  103 us (99%)
    pallas_call x1, Pallas kernels, on_device(): pl.pallas_call(kernel, out_shape=tuple((pltpu.VMEM(s, BF) for s in shapes...  101 us
    pallas_call x1, Pallas kernels, on_device(): pl.pallas_call(write_out, out_shape=tuple((jax.ShapeDtypeStruct(s, BF) fo...  2.49 us

profile of v2, /device:TPU:4, one launch (start us, length us, event | category | flops | bytes accessed | tf_op | source)
XLA Modules:
  0.0 104.1 jit_solution(5784342449843957458)
XLA Ops:
  0.6 100.9 %ffn_grad.1 = (bf16[32,1024]{1,0:T(8,128)(2,1)S(1)}, bf16[1024,896]{1,0:T(8,128)(2,1)S(1)}, bf16[1024,896]{1,0:T(8,128)(2,1)S(1)}, bf16[896,1024]{1,0:T(8,128)(2,1)S(1)}) custom-call(bf16[32,1024]{1,0:T(8,128)(2,1)} %x_h.1, bf16[32,1024]{1,0:T(8,128)(2,1)} %og_h.1, bf16[128,896]{1,0:T(8,128)(2,1)} %g_h.1, bf16[128,896]{1,0:T(8,128)(2,1)} %u_h.1, ...), custom_call_target="tpu_custom_call" | custom-call | tf_op jit(solution)/shard_map/ffn_grad/pallas_call | solution.py:492
  101.6 2.5 %write_out.1 = (bf16[32,1024]{1,0:T(8,128)(2,1)}, bf16[1024,896]{1,0:T(8,128)(2,1)}, bf16[1024,896]{1,0:T(8,128)(2,1)}, bf16[896,1024]{1,0:T(8,128)(2,1)}) custom-call(bf16[32,1024]{1,0:T(8,128)(2,1)S(1)} %get-tuple-element.8.refs_0_, bf16[1024,896]{1,0:T(8,128)(2,1)S(1)} %get-tuple-element.9.refs_1_, bf16[1024,896]{1,0:T(8,128)(2,1)S(1)} %get-tuple-element.10.refs_2_, ...), custom_call_target="tpu_custom_call" | custom-call | tf_op jit(solution)/shard_map/write_out/pallas_call | solution.py:534

commit v3 on v2

--- a/solution.py
+++ b/solution.py
@@ -33,7 +33,7 @@
 ):
     z, col = lax.axis_index("row"), lax.axis_index("col")
     chip, core = col // 2, lax.rem(col, 2)
-    cx = chip // 4
+    cx, cy = chip // 4, lax.rem(chip, 4)
     sib = (z, col + 1 - 2 * core)
 
     def zdev(d):
@@ -121,7 +121,61 @@
 
         lax.fori_loop(0, NCHIP, body, 0)
 
-    ogx, xx = (og, og_s, og_r, ogc_s, ogc_r), (xa, x_s, x_r, xc_s, xc_r)
+    xx = (xa, x_s, x_r, xc_s, xc_r)
+
+    def chip_xy(dx, dy):
+        return lax.rem(cx + dx + 4, 4) * 4 + lax.rem(cy + dy + 4, 4)
+
+    def og_rows(dx, dy, h):
+        return og.at[pl.ds(pl.multiple_of((2 * chip_xy(-dx, -dy) + core) * PR + h * 16, 16), 16)]
+
+    def og_copy(h, dx, dy):
+        if h == 0:
+            p, to = og_rows(dx if dy else 0, 0, 0), (0, dy) if dy else (dx, 0)
+        else:
+            p, to = og_rows(0, dy if dx else 0, 1), (dx, 0) if dx else (0, dy)
+        j = 4 * dx + dy
+        return remote(p, p, og_s.at[h, j], og_r.at[h, j], (z, 2 * chip_xy(*to) + core))
+
+    def og_wait(h, dx, dy):
+        p, j = og_rows(dx, dy, h), 4 * dx + dy
+        remote(p, p, og_s.at[h, j], og_r.at[h, j], sib).wait_recv()
+
+    def og_share(dx, dy, their):
+        c = 2 * chip_xy(-dx, -dy) + (1 - core if their else core)
+        p, j = og.at[pl.ds(pl.multiple_of(c * PR, PR), PR)], 4 * dx + dy
+        return remote(p, p, ogc_s.at[j], ogc_r.at[j], sib)
+
+    FAR = (1, 3, 2)
+    OFFSETS = [(dx, dy) for dx in range(4) for dy in range(4)]
+
+    def og_start():
+        for n in FAR:
+            og_copy(0, n, 0).start()
+            og_copy(1, 0, n).start()
+        og_share(0, 0, False).start()
+        for n in FAR:
+            og_copy(0, 0, n).start()
+            og_copy(1, n, 0).start()
+
+    def og_turn():
+        for n in FAR:
+            og_wait(0, n, 0)
+            for m in FAR:
+                og_copy(0, n, m).start()
+            og_wait(1, 0, n)
+            for m in FAR:
+                og_copy(1, m, n).start()
+
+    def og_finish(offsets):
+        for dx, dy in offsets:
+            if dy:
+                og_wait(0, dx, dy)
+            if dx:
+                og_wait(1, dx, dy)
+            if dx or dy:
+                og_share(dx, dy, False).start()
+
 
     G, U, UP, GD, UD, ACT = range(6)
     low, high = pl.ds(0, HT), pl.ds(HT, HT)
@@ -163,7 +217,7 @@
     locals_[1].wait()
     ring_send(U)
     locals_[2].wait()
-    send_own(*ogx)
+    og_start()
 
     def silu_parts(g, u):
         s = jax.nn.sigmoid(g)
@@ -186,15 +240,14 @@
     tiles(own_act)
 
     ring_send(ACT)
+    og_turn()
     ring_take(G, 1)
     ring_take(U, 1)
-    pass_on(1, 4, *ogx)
+    og_finish(OFFSETS[:8])
     ring_take(ACT, 1)
-    pass_on(4, 10, *ogx)
-    ring_take(G, 2)
-    pass_on(10, NCHIP, *ogx)
-    ring_take(U, 2)
-    wait_shared(og, ogc_s, ogc_r)
+    og_finish(OFFSETS[8:])
+    for n in OFFSETS:
+        og_share(*n, True).wait_recv()
 
     def rows(b):
         return pl.ds(pl.multiple_of(b * TB, TB), TB)
@@ -266,21 +319,19 @@
     locals_[6].wait()
     make_terms([4])
     rs_step(1, True)
+    ring_take(G, 2)
     make_terms([3, 5, 2, 6])
     rs_step(2, True)
-    ring_take(G, 3)
+    ring_take(U, 2)
+    rs_step(2, False)
     locals_[5].wait()
     send_own(*xx)
-    rs_step(2, False)
-    ring_take(U, 3)
     make_terms([1, 7, 0])
     rs_step(3, False)
-    ring_take(G, 4)
-    ring_take(U, 4)
     rs_step(4, False)
-    ring_take(ACT, 2)
+    ring_take(G, 3)
+    ring_take(U, 3)
     pass_on(1, NCHIP, *xx)
-    all_act(0, 8)
 
     for d in (0, 1):
         for q in (0, 1):
@@ -418,11 +469,16 @@
         sum_x(before)
         sum_cores(now)
         ring_take(UD, s + 1)
+        if s == 1:
+            ring_take(G, 4)
+            ring_take(U, 4)
+            all_act(0, 8)
         if s == 2:
-            ring_take(ACT, 3)
+            ring_take(ACT, 2)
     now = step_blocks(4)
     deltas(now)
     inputs(now)
+    ring_take(ACT, 3)
     sum_x(step_blocks(3))
     sum_cores(now)
     grads(now, False, True)
@@ -444,7 +500,8 @@
         gi[:, q * 256 : (q + 1) * 256] = t.astype(BF)
 
     def gone(j, _):
-        spread(og, j, og_s, og_r).wait_send()
+        remote(og_rows(0, 0, 0), og_rows(0, 0, 0), og_s.at[0, j], og_r.at[0, j], sib).wait_send()
+        remote(og_rows(0, 0, 0), og_rows(0, 0, 0), og_s.at[1, j], og_r.at[1, j], sib).wait_send()
         spread(xa, j, x_s, x_r).wait_send()
         remote(s2.at[0, pl.ds(0, PR)], rr.at[j], rr_s.at[j], rr_r.at[j], sib).wait_send()
         return 0
@@ -452,7 +509,7 @@
     lax.fori_loop(1, NCHIP, gone, 0)
 
     def gone_core(j, _):
-        share(og, j, ogc_s, ogc_r).wait_send()
+        remote(og.at[mine], og.at[mine], ogc_s.at[j], ogc_r.at[j], sib).wait_send()
         share(xa, j, xc_s, xc_r).wait_send()
         return 0
 
@@ -519,7 +576,7 @@
             pltpu.VMEM((NCHIP, PR, 256), BF),
             dma((9,)),
             *[dma((6, 2, 4))] * 2,
-            *plane, *plane,
+            *[dma((2, NCHIP))] * 2, *plane,
             *plane, *plane,
             *[dma((2, 4, 4))] * 2,
             *[dma((NZ,))] * 2,

time: 104 us -> 99.3 us (0.955)
  Pallas kernels: 103 us -> 98.6 us
    pallas_call x1, Pallas kernels: 101 us -> 96.1 us  [on_device(): pl.pallas_call(kernel, out_shape=tuple((pltpu.VMEM(s, BF) for s in shapes...]
where the time goes in v3:
time: 99.3 us; the launch traced here: 99.2 us
  Pallas kernels  98.6 us (99%)
    pallas_call x1, Pallas kernels, on_device(): pl.pallas_call(kernel, out_shape=tuple((pltpu.VMEM(s, BF) for s in shapes...  96.1 us
    pallas_call x1, Pallas kernels, on_device(): pl.pallas_call(write_out, out_shape=tuple((jax.ShapeDtypeStruct(s, BF) fo...  2.49 us

profile of v3, /device:TPU:4, one launch (start us, length us, event | category | flops | bytes accessed | tf_op | source)
XLA Modules:
  0.0 99.2 jit_solution(376832720525255029)
XLA Ops:
  0.6 96.1 %ffn_grad.1 = (bf16[32,1024]{1,0:T(8,128)(2,1)S(1)}, bf16[1024,896]{1,0:T(8,128)(2,1)S(1)}, bf16[1024,896]{1,0:T(8,128)(2,1)S(1)}, bf16[896,1024]{1,0:T(8,128)(2,1)S(1)}) custom-call(bf16[32,1024]{1,0:T(8,128)(2,1)} %x_h.1, bf16[32,1024]{1,0:T(8,128)(2,1)} %og_h.1, bf16[128,896]{1,0:T(8,128)(2,1)} %g_h.1, bf16[128,896]{1,0:T(8,128)(2,1)} %u_h.1, ...), custom_call_target="tpu_custom_call" | custom-call | tf_op jit(solution)/shard_map/ffn_grad/pallas_call | solution.py:549
  96.7 2.5 %write_out.1 = (bf16[32,1024]{1,0:T(8,128)(2,1)}, bf16[1024,896]{1,0:T(8,128)(2,1)}, bf16[1024,896]{1,0:T(8,128)(2,1)}, bf16[896,1024]{1,0:T(8,128)(2,1)}) custom-call(bf16[32,1024]{1,0:T(8,128)(2,1)S(1)} %get-tuple-element.8.refs_0_, bf16[1024,896]{1,0:T(8,128)(2,1)S(1)} %get-tuple-element.9.refs_1_, bf16[1024,896]{1,0:T(8,128)(2,1)S(1)} %get-tuple-element.10.refs_2_, ...), custom_call_target="tpu_custom_call" | custom-call | tf_op jit(solution)/shard_map/write_out/pallas_call | solution.py:591

commit v4 on v3

--- a/solution.py
+++ b/solution.py
@@ -478,9 +478,9 @@
     now = step_blocks(4)
     deltas(now)
     inputs(now)
+    sum_cores(now)
+    sum_x(step_blocks(3))
     ring_take(ACT, 3)
-    sum_x(step_blocks(3))
-    sum_cores(now)
     grads(now, False, True)
     sum_x(now)
     ring_take(ACT, 4)

time: 99.3 us -> 98.1 us (0.988)
  Pallas kernels: 98.6 us -> 96.8 us
    pallas_call x1, Pallas kernels: 96.1 us -> 94.3 us  [on_device(): pl.pallas_call(kernel, out_shape=tuple((pltpu.VMEM(s, BF) for s in shapes...]
where the time goes in v4:
time: 98.1 us; the launch traced here: 97.5 us
  Pallas kernels  96.8 us (99%)
    pallas_call x1, Pallas kernels, on_device(): pl.pallas_call(kernel, out_shape=tuple((pltpu.VMEM(s, BF) for s in shapes...  94.3 us
    pallas_call x1, Pallas kernels, on_device(): pl.pallas_call(write_out, out_shape=tuple((jax.ShapeDtypeStruct(s, BF) fo...  2.49 us

profile of v4, /device:TPU:4, one launch (start us, length us, event | category | flops | bytes accessed | tf_op | source)
XLA Modules:
  0.0 97.5 jit_solution(14976146170751940769)
XLA Ops:
  0.6 94.3 %ffn_grad.1 = (bf16[32,1024]{1,0:T(8,128)(2,1)S(1)}, bf16[1024,896]{1,0:T(8,128)(2,1)S(1)}, bf16[1024,896]{1,0:T(8,128)(2,1)S(1)}, bf16[896,1024]{1,0:T(8,128)(2,1)S(1)}) custom-call(bf16[32,1024]{1,0:T(8,128)(2,1)} %x_h.1, bf16[32,1024]{1,0:T(8,128)(2,1)} %og_h.1, bf16[128,896]{1,0:T(8,128)(2,1)} %g_h.1, bf16[128,896]{1,0:T(8,128)(2,1)} %u_h.1, ...), custom_call_target="tpu_custom_call" | custom-call | tf_op jit(solution)/shard_map/ffn_grad/pallas_call | solution.py:549
  95.0 2.5 %write_out.1 = (bf16[32,1024]{1,0:T(8,128)(2,1)}, bf16[1024,896]{1,0:T(8,128)(2,1)}, bf16[1024,896]{1,0:T(8,128)(2,1)}, bf16[896,1024]{1,0:T(8,128)(2,1)}) custom-call(bf16[32,1024]{1,0:T(8,128)(2,1)S(1)} %get-tuple-element.8.refs_0_, bf16[1024,896]{1,0:T(8,128)(2,1)S(1)} %get-tuple-element.9.refs_1_, bf16[1024,896]{1,0:T(8,128)(2,1)S(1)} %get-tuple-element.10.refs_2_, ...), custom_call_target="tpu_custom_call" | custom-call | tf_op jit(solution)/shard_map/write_out/pallas_call | solution.py:591
